TPU v7x, 256 devices: a whole 4x4x8 slice. The times are simulated.
256 devices in a mesh: section: 64 (over z_lo, y, x), tensor: 4 (over z_hi, core).
Axes of the slice: x: 4, y: 4, z: 8 (z_hi: 2, z_lo: 4; z = z_hi * 4 + z_lo), core: 2. Of those that a mesh axis runs over, the one named last changes fastest.
Arguments:
- queries: bfloat16 [8192, 16384], P('section', 'tensor'), may hold values from -108 to 108
- new_keys: bfloat16 [8192, 1024], P('section', 'tensor'), may hold values from -10 to 10
- new_values: bfloat16 [8192, 1024], P('section', 'tensor'), may hold values from -6 to 6
- cache_keys: bfloat16 [65536, 1024], P('section', 'tensor'), may hold values from -6 to 6
- cache_values: bfloat16 [65536, 1024], P('section', 'tensor'), may hold values from -6 to 6
- prior_length: int32 [64], P('section'), may hold values from 1 to 1024, as said below
- placement: int32 [1024, 1], P('section'), may hold values from 0 to 63; in each aligned block of 16 rows (0 to 15, 16 to 31, ...) at most 2 rows name the same one
Outputs:
- handed: bfloat16 [8192, 16384], P(('section', 'tensor'))
- landed: bfloat16 [8192, 8, 2, 1024], P('section', None, None, 'tensor')
Inputs may be any that keep to these rules, and one draw needn't show every extreme that they name: `prior_length`: some section has exactly 1024 live cache slots. `placement`: of the 16 blocks of one section, at most 2 go to one destination section, and some destination gets exactly 2.
All inputs are finite; a program needn't handle non-finite values.
Results may differ from a plain program's by a relative error of at most 0.012.
The roundings to bfloat16 on the way count: a program that leaves them out, or rounds other values in their place, can miss the bound.
Values may be sent and summed in bfloat16 or wider, within the bound.
A program may use at most 64 MiB of HBM per device.

v0:
```python
import jax
import jax.numpy as jnp
from jax import lax
from jax.sharding import PartitionSpec as P

HEAD = 128
ROW_BLOCK = 128
BLOCK_TOK = 8


def passed_along(block, axis, distance):
    devices = range(lax.axis_size(axis))
    route = [((i - distance) % len(devices), i) for i in devices]
    return lax.ppermute(block, axis, route)


def rotate(values, angles):
    half = values.shape[-1] // 2
    cosine = jnp.cos(angles)
    sine = jnp.sin(angles)
    first = values[..., :half]
    second = values[..., half:]
    return jnp.concatenate(
        [first * cosine - second * sine, second * cosine + first * sine], axis=-1
    )


def angle_table(start, count):
    index = jnp.arange(HEAD // 2, dtype=jnp.float32)
    frequency = jnp.exp(index * (-2.0 / HEAD) * jnp.log(jnp.float32(500000.0)))
    positions = start.astype(jnp.float32) + jnp.arange(count, dtype=jnp.float32)
    return positions[:, None] * frequency[None, :]


def pass_on(rows_out):
    return passed_along(rows_out, "section", 1)


def regroup(rows_out):
    return lax.all_to_all(rows_out, "tensor", split_axis=0, concat_axis=1, tiled=True)


def local(queries, new_keys, new_values, cache_keys, cache_values, prior_length, placement):
    rows = queries.shape[0]
    kv_width = new_keys.shape[1]
    groups = kv_width // HEAD
    group = queries.shape[1] // kv_width
    cache_slots = cache_keys.shape[0]
    length = prior_length[0]
    angles = angle_table(length, rows)
    keys_rotated = rotate(
        new_keys.astype(jnp.float32).reshape(rows, groups, HEAD), angles[:, None, :]
    )
    keys_rotated = keys_rotated.astype(jnp.bfloat16).reshape(rows, kv_width)
    sections = lax.axis_size("section")
    scale = HEAD ** (-0.5)
    cache_valid = (jnp.arange(cache_slots) < length)[None, None, :]
    causal = (jnp.arange(rows)[None, :] <= (0 + jnp.arange(ROW_BLOCK))[:, None])[None]
    head_outputs = []
    for index_head in range(groups):
        query_part = queries[
            0:ROW_BLOCK, index_head * group * HEAD : (index_head + 1) * group * HEAD
        ]
        query_part = query_part.astype(jnp.float32).reshape(ROW_BLOCK, group, HEAD)
        query_part = rotate(query_part, angles[:, None, :]).astype(jnp.bfloat16)
        flat = jnp.transpose(query_part, (1, 0, 2)).reshape(group * ROW_BLOCK, HEAD)
        column = slice(index_head * HEAD, (index_head + 1) * HEAD)
        cache_scores = jnp.einsum(
            "rh,kh->rk", flat, cache_keys[:, column], preferred_element_type=jnp.float32
        )
        span_scores = jnp.einsum(
            "rh,kh->rk", flat, keys_rotated[:, column], preferred_element_type=jnp.float32
        )
        cache_scores = jnp.where(
            cache_valid, (cache_scores * scale).reshape(group, ROW_BLOCK, cache_slots), -1e30
        )
        span_scores = jnp.where(
            causal, (span_scores * scale).reshape(group, ROW_BLOCK, rows), -1e30
        )
        top = jnp.maximum(
            jnp.max(cache_scores, axis=-1, keepdims=True),
            jnp.max(span_scores, axis=-1, keepdims=True),
        )
        cache_weights = jnp.where(cache_valid, jnp.exp(cache_scores - top), 0.0)
        span_weights = jnp.where(causal, jnp.exp(span_scores - top), 0.0)
        total = jnp.sum(cache_weights, axis=-1, keepdims=True) + jnp.sum(
            span_weights, axis=-1, keepdims=True
        )
        cache_rounded = cache_weights.astype(jnp.bfloat16).reshape(group * ROW_BLOCK, cache_slots)
        span_rounded = span_weights.astype(jnp.bfloat16).reshape(group * ROW_BLOCK, rows)
        summed = jnp.dot(cache_rounded, cache_values[:, column], preferred_element_type=jnp.float32)
        summed = summed + jnp.dot(
            span_rounded, new_values[:, column], preferred_element_type=jnp.float32
        )
        summed = summed.reshape(group, ROW_BLOCK, HEAD) / total
        head_outputs.append(
            jnp.transpose(summed, (1, 0, 2)).reshape(ROW_BLOCK, group * HEAD).astype(jnp.bfloat16)
        )
    pieces = jnp.concatenate(head_outputs, axis=1)
    handed = pass_on(regroup(pieces))
    count = rows // BLOCK_TOK
    most = max(2, 2 * count // sections)
    target = placement[:, 0]
    onehot = (target[:, None] == jnp.arange(sections, dtype=jnp.int32)[None, :]).astype(jnp.int32)
    earlier = jnp.cumsum(onehot, axis=0) - onehot
    slot = jnp.sum(earlier * onehot, axis=1)
    index = target * most + slot
    blocks = jnp.stack([keys_rotated, new_values], axis=1).reshape(count, BLOCK_TOK, 2, kv_width)
    outgoing = (
        jnp.zeros((sections * most, BLOCK_TOK, 2, kv_width), jnp.bfloat16).at[index].set(blocks)
    )
    landed = lax.all_to_all(outgoing, "section", split_axis=0, concat_axis=0, tiled=True)
    return (handed, landed)


def solution(mesh):
    placed = (
        P("section", "tensor"),
        P("section", "tensor"),
        P("section", "tensor"),
        P("section", "tensor"),
        P("section", "tensor"),
        P("section"),
        P("section", None),
    )
    return jax.shard_map(
        local,
        mesh=mesh,
        in_specs=placed,
        out_specs=(P(("section", "tensor"), None), P("section", None, None, "tensor")),
        check_vma=False,
    )
```

profile of v0, /device:TPU:1, one launch (start us, length us, event | category | flops | bytes accessed | tf_op | source)
XLA Modules:
  0.0 132.2 jit_solution(11996722110122341165)
XLA Ops:
  1.3 1.3 fusion.50
  2.6 0.3 copy.28
  2.9 0.1 convert.19
  3.0 0.3 copy.29
  3.3 0.1 convert.20
  3.4 0.2 multiply_cosine_fusion
  3.6 0.1 copy.17
  3.7 0.1 copy.18
  3.8 0.3 subtract_convert_fusion.1
  4.1 0.1 maximum_bitcast_fusion
  4.2 0.3 copy.16
  4.5 0.1 reshape.240
  4.6 0.3 multiply_subtract_fusion
  4.9 0.2 maximum_convert_fusion
  5.1 0.6 iota_compare_fusion.2
  5.7 0.3 copy.22
  6.0 0.1 broadcast_in_dim.90
  6.1 0.4 fusion.51
  6.5 1.1 fusion.52
  7.6 2.7 %fusion = (f32[2048]{0:T(1024)S(1)}, f32[2048,1024]{0,1:T(8,128)S(1)}) fusion(pred[1024]{0:T(1024)(128)(4,1)} %iota_compare_fusion.2, bf16[2048,128]{1,0:T(8,128)(2,1)S(1)} %bitcast.71, bf16[1024,256]{1,0:T(8,128)(2,1)} %param.10), kind=kOutput, calls=%fused_computation.5 | convolution fusion | flops 543160320 | bytes 9184256 | tf_op jit(solution)/shard_map/rh,kh->rk/dot_general | solution.py:68
  10.3 3.6 %fusion.2 = (f32[2048]{0:T(1024)S(1)}, f32[2048]{0:T(1024)S(1)}, f32[2048,1024]{0,1:T(8,128)S(1)}) fusion(f32[2048,1024]{0,1:T(8,128)S(1)} %get-tuple-element.25, f32[2048]{0:T(1024)S(1)} %max.16, pred[1024]{0:T(1024)(128)(4,1)S(1)} %copy-done.4, bf16[2048,128]{1,0:T(8,128)(2,1)S(1)} %bitcast.77, bf16[1024,256]{1,0:T(8,128)(2,1)S(1)} %copy-done.1), kind=kOutput, calls=%fused_computation.7 | convolution fusion | flops 553644032 | bytes 17589248 | tf_op jit(solution)/shard_map/rh,kh->rk/dot_general | solution.py:68
  13.9 2.6 %fusion.8 = f32[2048,128]{1,0:T(8,128)S(1)} fusion(f32[2048,1024]{0,1:T(8,128)S(1)} %get-tuple-element.25, f32[2048]{0:T(1024)S(1)} %max.16, pred[1024]{0:T(1024)(128)(4,1)S(1)} %copy-done.4, bf16[1024,256]{1,0:T(8,128)(2,1)S(1)} %copy-done.6), kind=kOutput, calls=%fused_computation.12 | convolution fusion | flops 547356672 | bytes 9708544 | tf_op jit(solution)/shard_map/dot_general | solution.py:91
  16.5 3.6 %fusion.6 = f32[2048,128]{1,0:T(8,128)} fusion(f32[2048,1024]{0,1:T(8,128)S(1)} %get-tuple-element.28, f32[2048]{0:T(1024)S(1)} %max.17, pred[1024]{0:T(1024)(128)(4,1)S(1)} %copy-done.4, bf16[1024,256]{1,0:T(8,128)(2,1)S(1)} %copy-done.6), kind=kOutput, calls=%fused_computation.11 | convolution fusion | flops 547356672 | bytes 9708544 | tf_op jit(solution)/shard_map/dot_general | solution.py:91
  20.1 3.5 %fusion.4 = f32[2048]{0:T(1024)} fusion(f32[2048,1024]{0,1:T(8,128)S(1)} %get-tuple-element.28, f32[2048]{0:T(1024)S(1)} %max.17, pred[1024]{0:T(1024)(128)(4,1)S(1)} %copy-done.4), kind=kLoop, calls=%fused_computation.9 | loop fusion | flops 10483712 | bytes 8406016 | tf_op jit(solution)/shard_map/reduce_sum | solution.py:86
  23.6 1.0 fusion.16
  24.6 0.6 add_bitcast_fusion.1
  25.2 1.4 %copy.19 = f32[16,128]{0,1:T(8,128)} copy(f32[16,128]{1,0:T(8,128)} %add_bitcast_fusion.1) | data formatting | bytes 16384 | tf_op jit(solution)/shard_map/add | solution.py:86
  26.7 0.5 convolution_add_fusion.1
  27.2 1.5 %fusion.26 = bf16[128,16,128]{2,1,0:T(8,128)(2,1)S(1)} fusion(f32[16,128]{0,1:T(8,128)} %copy.19, f32[16,128,128]{2,1,0:T(8,128)S(1)} %bitcast.64), kind=kLoop, calls=%fused_computation.42 | loop fusion | flops 524288 | bytes 1581056 | tf_op jit(solution)/shard_map/convert_element_type | solution.py:97
  28.7 0.2 convert_element_type.72
  29.0 1.7 %convolution_add_fusion = f32[2048,128]{1,0:T(8,128)S(1)} fusion(f32[2048,128]{1,0:T(8,128)} %fusion.6, f32[2048,128]{0,1:T(8,128)S(1)} %get-tuple-element.30, f32[2048]{0:T(1024)S(1)} %max.17, bf16[128,256]{1,0:T(8,128)(2,1)S(1)} %copy-done, pred[16,8,16,128]{3,2,1,0:T(8,128)(4,1)S(1)} %bitcast.69), kind=kOutput, calls=%fused_computation.15 | convolution fusion | flops 68157440 | bytes 3448832 | tf_op jit(solution)/shard_map/dot_general | solution.py:92
  30.7 0.7 add_bitcast_fusion
  31.4 0.1 copy.23
  31.5 0.7 fusion.27
  32.2 0.2 convert_element_type.77
  32.4 1.1 pad_maximum_fusion
  33.5 10.0 %all-to-all-start = ((bf16[4,32,4096]{2,1,0:T(8,128)(2,1)}), bf16[4,32,4096]{2,1,0:T(8,128)(2,1)S(1)}, u32[]{:S(2)}, u32[]{:S(2)}) async-start(bf16[4,32,4096]{2,1,0:T(8,128)(2,1)} %pad_maximum_fusion), calls=%async_computation | async-start | bytes 2097152 | tf_op jit(solution)/shard_map/all_to_all | solution.py:40
  43.5 0.1 fusion.38
  43.6 0.2 select_reduce_fusion
  43.9 1.0 broadcast_in_dim.95
  44.9 2.2 %scatter_fusion = bf16[128,8,2,256]{3,1,2,0:T(8,128)(2,1)} fusion(bf16[128,8,2,256]{3,1,2,0:T(8,128)(2,1)} %broadcast_in_dim.95, s32[16]{0:T(128)S(1)} %fusion.39, bf16[16,8,2,256]{3,1,2,0:T(8,128)(2,1)S(1)} %pad_maximum_fusion.1), kind=kCustom, calls=%fused_computation | custom fusion | bytes 393280 | tf_op jit(solution)/shard_map/scatter | solution.py:110
  47.1 16.1 %all-to-all-done = bf16[4,32,4096]{2,1,0:T(8,128)(2,1)S(1)} async-done(((bf16[4,32,4096]{2,1,0:T(8,128)(2,1)}), bf16[4,32,4096]{2,1,0:T(8,128)(2,1)S(1)}, u32[]{:S(2)}, u32[]{:S(2)}) %all-to-all-start) | async-done | bytes 1048608 | tf_op jit(solution)/shard_map/all_to_all | solution.py:40
  63.2 17.5 %all-to-all-start.1 = ((bf16[128,8,2,256]{3,1,2,0:T(8,128)(2,1)}), bf16[128,8,2,256]{3,1,2,0:T(8,128)(2,1)S(1)}, u32[]{:S(2)}, u32[]{:S(2)}) async-start(bf16[128,8,2,256]{3,1,2,0:T(8,128)(2,1)} %scatter_fusion), calls=%async_computation.1 | async-start | bytes 2097152 | tf_op jit(solution)/shard_map/all_to_all | solution.py:112
  80.7 0.1 copy.30
  80.8 1.1 collective-permute-start
  81.9 47.5 %all-to-all-done.1 = bf16[128,8,2,256]{3,1,2,0:T(8,128)(2,1)S(1)} async-done(((bf16[128,8,2,256]{3,1,2,0:T(8,128)(2,1)}), bf16[128,8,2,256]{3,1,2,0:T(8,128)(2,1)S(1)}, u32[]{:S(2)}, u32[]{:S(2)}) %all-to-all-start.1) | async-done | bytes 1048608 | tf_op jit(solution)/shard_map/all_to_all | solution.py:112
  129.4 1.8 %copy.27 = bf16[128,8,2,256]{3,2,1,0:T(2,128)(2,1)} copy(bf16[128,8,2,256]{3,1,2,0:T(8,128)(2,1)S(1)} %all-to-all-done.1) | data formatting | bytes 2097152
  131.2 1.0 copy.60
  (25 shorter events, 0.2 us)
Async XLA Ops:
  0.6 3.9 %copy-start.2 = (bf16[128,256]{1,0:T(8,128)(2,1)S(1)}, bf16[128,256]{1,0:T(8,128)(2,1)}, u32[]{:S(2)}) copy-start(bf16[128,256]{1,0:T(8,128)(2,1)} %param.8) | copy-start | bytes 196612
  5.1 1.3 %copy-start.3 = (bf16[16,8,2,128]{3,1,2,0:T(8,128)(2,1)}, bf16[16,8,2,128]{3,1,2,0:T(8,128)(2,1)S(1)}, u32[]{:S(2)}) copy-start(bf16[16,8,2,128]{3,1,2,0:T(8,128)(2,1)S(1)} %copy.56) | copy-start | bytes 196612
  6.0 4.3 %copy-start.1 = (bf16[1024,256]{1,0:T(8,128)(2,1)S(1)}, bf16[1024,256]{1,0:T(8,128)(2,1)}, u32[]{:S(2)}) copy-start(bf16[1024,256]{1,0:T(8,128)(2,1)} %param.10) | copy-start | bytes 1572868
  6.1 4.3 %copy-start.4 = (pred[1024]{0:T(1024)(128)(4,1)S(1)}, pred[1024]{0:T(1024)(128)(4,1)}, u32[]{:S(2)}) copy-start(pred[1024]{0:T(1024)(128)(4,1)} %iota_compare_fusion.2) | copy-start | bytes 3076
  10.3 3.6 %copy-start.6 = (bf16[1024,256]{1,0:T(8,128)(2,1)S(1)}, bf16[1024,256]{1,0:T(8,128)(2,1)}, u32[]{:S(2)}) copy-start(bf16[1024,256]{1,0:T(8,128)(2,1)} %param.11) | copy-start | bytes 1572868
  20.1 6.6 %copy-start = (bf16[128,256]{1,0:T(8,128)(2,1)S(1)}, bf16[128,256]{1,0:T(8,128)(2,1)}, u32[]{:S(2)}) copy-start(bf16[128,256]{1,0:T(8,128)(2,1)} %param.9) | copy-start | bytes 196612
  27.2 16.4 %copy-start.5 = (s32[16,1]{0,1:T(1,128)S(1)}, s32[16,1]{0,1:T(1,128)}, u32[]{:S(2)}) copy-start(s32[16,1]{0,1:T(1,128)} %param.13) | copy-start | bytes 196
  33.5 29.7 %all-to-all-start = ((bf16[4,32,4096]{2,1,0:T(8,128)(2,1)}), bf16[4,32,4096]{2,1,0:T(8,128)(2,1)S(1)}, u32[]{:S(2)}, u32[]{:S(2)}) async-start(bf16[4,32,4096]{2,1,0:T(8,128)(2,1)} %pad_maximum_fusion), calls=%async_computation | async-start | bytes 2097152 | tf_op jit(solution)/shard_map/all_to_all | solution.py:40
  63.2 66.2 %all-to-all-start.1 = ((bf16[128,8,2,256]{3,1,2,0:T(8,128)(2,1)}), bf16[128,8,2,256]{3,1,2,0:T(8,128)(2,1)S(1)}, u32[]{:S(2)}, u32[]{:S(2)}) async-start(bf16[128,8,2,256]{3,1,2,0:T(8,128)(2,1)} %scatter_fusion), calls=%async_computation.1 | async-start | bytes 2097152 | tf_op jit(solution)/shard_map/all_to_all | solution.py:112
  80.8 50.4 %collective-permute-start = (bf16[32,16384]{1,0:T(8,128)(2,1)S(1)}, bf16[32,16384]{1,0:T(8,128)(2,1)S(1)}, u32[]{:S(2)}, u32[]{:S(2)}) collective-permute-start(bf16[32,16384]{1,0:T(8,128)(2,1)S(1)} %bitcast.74), channel_id=1, source_target_pairs={{252,0},{0,4},{4,8},{8,12},{12,16},{16,20},{20,24},{24,28},{28,32}... | collective-permute-start | bytes 3145736 | tf_op jit(solution)/shard_map/ppermute | solution.py:14
where the time goes:
time: 134 us; the launch traced here: 132 us
  waiting for transfers between devices  63.6 us (47%)
  starting transfers between devices  28.5 us (21%)
  matrix products  16.1 us (12%)
  other arithmetic  11.4 us (9%)
  local copies, waits for them, and re-layouts  10.9 us (8%)
  between operations  1.65 us (1%)
    all_to_all x1, waiting for transfers between devices, local(): lax.all_to_all(outgoing, 'section', split_axis=0, concat_axis=0, tiled=True)  47.5 us
    all_to_all x1, starting transfers between devices, local(): lax.all_to_all(outgoing, 'section', split_axis=0, concat_axis=0, tiled=True)  17.5 us
    all_to_all x1, waiting for transfers between devices, regroup(): lax.all_to_all(rows_out, 'tensor', split_axis=0, concat_axis=1, tiled=True)  16.1 us
    all_to_all x1, starting transfers between devices, regroup(): lax.all_to_all(rows_out, 'tensor', split_axis=0, concat_axis=1, tiled=True)  9.96 us
    dot_general x2, matrix products, local(): jnp.einsum('rh,kh->rk', flat, cache_keys[:, column], preferred_element_ty...  6.27 us
    dot_general x2, matrix products, local(): jnp.dot(cache_rounded, cache_values[:, column], preferred_element_type=jn...  6.15 us
    reduce_sum x1, other arithmetic, local(): jnp.sum(cache_weights, axis=-1, keepdims=True)  3.51 us
    unnamed x19, local copies, waits for them, and re-layouts  3.38 us
  transfers between devices with their start and end apart: 3, of which 2 were waited for; matrix products, arithmetic and copies ran while one was open for 4% of the time, Pallas kernels for 0%

commit v1 on v0

v1 whole, which is shorter than its diff:
```python
import functools

import jax
import jax.numpy as jnp
from jax import lax
from jax.experimental import pallas as pl
from jax.experimental.pallas import tpu as pltpu
from jax.sharding import PartitionSpec as P

MESH = pl.DeviceIdType.MESH
HEAD = 128
ROWS = 128
CACHE = 1024
BLOCK_TOK = 8
PLANE = 16
DEPTH = 4
TENSOR = 4
HEADS = 32
STEP_HEADS = 4
STEPS = HEADS // STEP_HEADS
STEP_COLS = STEP_HEADS * HEAD
KV_WIDTH = 2 * HEAD
ROW_PART = ROWS // TENSOR
MASKED = -1e30


def kernel(
    queries, new_keys, new_values, cache_keys, cache_values, cosine, sine, bias, slots,
    handed, landed,
    attended, held, packed,
    in_send, in_recv, plane_send, plane_recv, own_sem, out_send, out_recv,
):
    section = lax.axis_index("section")
    tensor = lax.axis_index("tensor")
    sections = DEPTH * PLANE
    z, xy = section // PLANE, section % PLANE
    after = lax.rem(section + 1, sections)
    before = lax.rem(section + sections - 1, sections)

    barrier = pltpu.get_barrier_semaphore()

    def greet(device):
        pl.semaphore_signal(barrier, inc=1, device_id=device, device_id_type=MESH)

    for i in range(1, DEPTH):
        greet((lax.rem(z + i, DEPTH) * PLANE + xy, tensor))
    for i in range(TENSOR):
        greet((before, lax.rem(tensor + i, TENSOR)))

    @pl.loop(1, PLANE)
    def _(i):
        greet((z * PLANE + lax.rem(xy + i, PLANE), tensor))

    def rotate(part):
        part = part.astype(jnp.float32)
        turned = pltpu.roll(part, HEAD // 2, 1)
        return (part * cosine[...] + turned * sine[...]).astype(jnp.bfloat16)

    for g in range(2):
        columns = pl.ds(g * HEAD, HEAD)
        held[z, pl.ds(0, ROWS), columns] = rotate(new_keys[:, columns])
    held[z, pl.ds(0, ROWS), pl.ds(KV_WIDTH, KV_WIDTH)] = new_values[...]
    held[z, pl.ds(ROWS, 16), :] = slots[...]

    pl.semaphore_wait(barrier, DEPTH - 1 + TENSOR + PLANE - 1)

    for i in (2, 1, 3):
        pltpu.make_async_remote_copy(
            src_ref=held.at[z], dst_ref=held.at[z], send_sem=in_send, recv_sem=in_recv.at[z],
            device_id=(lax.rem(z + i, DEPTH) * PLANE + xy, tensor), device_id_type=MESH,
        ).start()

    def spread(source):
        row = lax.broadcasted_iota(jnp.int32, (PLANE * 16, ROWS), 0)
        column = lax.broadcasted_iota(jnp.int32, (PLANE * 16, ROWS), 1)
        slot = held[source, pl.ds(ROWS, 16), pl.ds(0, ROWS)].astype(jnp.float32)[0:1, :]
        wanted = (row // BLOCK_TOK + z * PLANE * 2).astype(jnp.float32)
        here = (slot == wanted) & (row % BLOCK_TOK == column % BLOCK_TOK)
        picked = jnp.where(here, 1.0, 0.0).astype(jnp.bfloat16)
        moved = jnp.dot(picked, held[source, pl.ds(0, ROWS), :], preferred_element_type=jnp.float32)
        packed[source] = moved.astype(jnp.bfloat16).reshape(PLANE, 16, 2 * KV_WIDTH)

        @pl.loop(1, PLANE)
        def _(i):
            other = lax.rem(xy + i, PLANE)
            pltpu.make_async_remote_copy(
                src_ref=packed.at[source, other], dst_ref=landed.at[source, xy],
                send_sem=plane_send, recv_sem=plane_recv,
                device_id=(z * PLANE + other, tensor), device_id_type=MESH,
            ).start()
        pltpu.make_async_copy(packed.at[source, xy], landed.at[source, xy], own_sem).start()

    spread(z)

    row = lax.broadcasted_iota(jnp.int32, (ROWS, ROWS), 0)
    column = lax.broadcasted_iota(jnp.int32, (ROWS, ROWS), 1)
    causal = column <= row
    sharp = HEAD ** (-0.5) * 1.4426950408889634

    @pl.loop(0, STEPS)
    def _(step):
        g = step // (STEPS // 2)
        key_columns = pl.ds(pl.multiple_of(g * HEAD, HEAD), HEAD)
        value_columns = pl.ds(pl.multiple_of(KV_WIDTH + g * HEAD, HEAD), HEAD)
        base = step * STEP_COLS
        dims = (((1,), (1,)), ((), ()))
        for h in range(STEP_HEADS):
            columns = pl.ds(pl.multiple_of(base + h * HEAD, HEAD), HEAD)
            query = rotate(queries[:, columns])
            old = lax.dot_general(query, cache_keys[:, key_columns], dims, preferred_element_type=jnp.float32)
            new = lax.dot_general(
                query, held[z, pl.ds(0, ROWS), key_columns], dims, preferred_element_type=jnp.float32
            )
            old = old + bias[...]
            new = jnp.where(causal, new, MASKED)
            top = jnp.maximum(jnp.max(old, axis=1, keepdims=True), jnp.max(new, axis=1, keepdims=True))
            old = jnp.exp2((old - top) * sharp)
            new = jnp.exp2((new - top) * sharp)
            total = jnp.sum(old, axis=1, keepdims=True) + jnp.sum(new, axis=1, keepdims=True)
            summed = jnp.dot(
                old.astype(jnp.bfloat16), cache_values[:, key_columns], preferred_element_type=jnp.float32
            ) + jnp.dot(
                new.astype(jnp.bfloat16), held[z, pl.ds(0, ROWS), value_columns],
                preferred_element_type=jnp.float32,
            )
            attended[:, columns] = (summed / total).astype(jnp.bfloat16)
        for i in (2, 3, 0, 1):
            part = lax.rem(tensor + i, TENSOR)
            pltpu.make_async_remote_copy(
                src_ref=attended.at[
                    pl.ds(pl.multiple_of(part * ROW_PART, ROW_PART), ROW_PART),
                    pl.ds(pl.multiple_of(base, STEP_COLS), STEP_COLS),
                ],
                dst_ref=handed.at[
                    :, pl.ds(pl.multiple_of(tensor * (HEADS * HEAD) + base, STEP_COLS), STEP_COLS)
                ],
                send_sem=out_send, recv_sem=out_recv,
                device_id=(after, part), device_id_type=MESH,
            ).start()

    for i in (1, 3, 2):
        source = lax.rem(z + i, DEPTH)
        pltpu.make_async_copy(held.at[source], held.at[source], in_recv.at[source]).wait()
        spread(source)

    def drain(ref, sem):
        pltpu.make_async_copy(ref, ref, sem).wait()

    drain(held.at[pl.ds(0, DEPTH - 1)], in_send)
    drain(packed.at[:, 0], own_sem)
    drain(packed.at[:, pl.ds(0, PLANE - 1)], plane_send)
    drain(landed.at[:, pl.ds(0, PLANE - 1)], plane_recv)
    drain(attended, out_send)
    drain(handed, out_recv)


def local(queries, new_keys, new_values, cache_keys, cache_values, prior_length, placement):
    length = prior_length[0]
    index = jnp.arange(HEAD // 2, dtype=jnp.float32)
    frequency = jnp.exp(index * (-2.0 / HEAD) * jnp.log(jnp.float32(500000.0)))
    positions = length.astype(jnp.float32) + jnp.arange(ROWS, dtype=jnp.float32)
    angles = positions[:, None] * frequency[None, :]
    cosine, sine = jnp.cos(angles), jnp.sin(angles)
    cosine = jnp.concatenate([cosine, cosine], axis=1)
    sine = jnp.concatenate([-sine, sine], axis=1)
    bias = jnp.where(jnp.arange(CACHE) < length, 0.0, MASKED).astype(jnp.float32)[None, :]
    target = placement[:, 0]
    order = jnp.arange(target.shape[0])
    earlier = (target[None, :] == target[:, None]) & (order[None, :] < order[:, None])
    slot = target * 2 + jnp.sum(earlier.astype(jnp.int32), axis=1)
    lanes = jnp.tile(jnp.repeat(slot, BLOCK_TOK), 2 * KV_WIDTH // ROWS).astype(jnp.bfloat16)
    slots = jnp.broadcast_to(lanes[None, :], (16, 2 * KV_WIDTH))

    vmem = pl.BlockSpec(memory_space=pltpu.VMEM)
    handed, landed = pl.pallas_call(
        kernel,
        out_shape=(
            jax.ShapeDtypeStruct((ROW_PART, TENSOR * HEADS * HEAD), jnp.bfloat16),
            jax.ShapeDtypeStruct((DEPTH, PLANE, 16, 2 * KV_WIDTH), jnp.bfloat16),
        ),
        in_specs=[vmem] * 9,
        out_specs=(vmem, vmem),
        scratch_shapes=[
            pltpu.VMEM((ROWS, HEADS * HEAD), jnp.bfloat16),
            pltpu.VMEM((DEPTH, ROWS + 16, 2 * KV_WIDTH), jnp.bfloat16),
            pltpu.VMEM((DEPTH, PLANE, 16, 2 * KV_WIDTH), jnp.bfloat16),
            pltpu.SemaphoreType.DMA,
            pltpu.SemaphoreType.DMA((DEPTH,)),
            pltpu.SemaphoreType.DMA,
            pltpu.SemaphoreType.DMA,
            pltpu.SemaphoreType.DMA,
            pltpu.SemaphoreType.DMA,
            pltpu.SemaphoreType.DMA,
        ],
        compiler_params=pltpu.CompilerParams(
            collective_id=0, has_side_effects=True, vmem_limit_bytes=40 << 20
        ),
        name="spanned",
    )(queries, new_keys, new_values, cache_keys, cache_values, cosine, sine, bias, slots)
    return handed, landed.reshape(DEPTH * PLANE * 2, BLOCK_TOK, 2, KV_WIDTH)


def solution(mesh):
    placed = (
        P("section", "tensor"),
        P("section", "tensor"),
        P("section", "tensor"),
        P("section", "tensor"),
        P("section", "tensor"),
        P("section"),
        P("section", None),
    )
    return jax.shard_map(
        local,
        mesh=mesh,
        in_specs=placed,
        out_specs=(P(("section", "tensor"), None), P("section", None, None, "tensor")),
        check_vma=False,
    )
```

time: 134 us -> 69.6 us (0.52)
  waiting for transfers between devices: 63.6 us -> 0 us
  Pallas kernels: 0 us -> 58.5 us
  starting transfers between devices: 28.5 us -> 0 us
  matrix products: 16.1 us -> 0 us
  other arithmetic: 11.4 us -> 2.01 us
  local copies, waits for them, and re-layouts: 10.9 us -> 6.91 us
    all_to_all x2 -> x0, waiting for transfers between devices: 63.6 us -> none  [the longest x1 47.5 us: local(): lax.all_to_all(outgoing, 'section', split_axis=0, concat_axis=0, tiled=True)]
    pallas_call x0 -> x1, Pallas kernels: none -> 58.5 us  [local(): pl.pallas_call(kernel, out_shape=(jax.ShapeDtypeStruct((ROW_PART, TENSOR...]
    all_to_all x2 -> x0, starting transfers between devices: 27.4 us -> none  [the longest x1 17.5 us: local(): lax.all_to_all(outgoing, 'section', split_axis=0, concat_axis=0, tiled=True)]
    dot_general x8 -> x0, matrix products: 16.1 us -> none  [the longest x2 6.27 us: local(): jnp.einsum('rh,kh->rk', flat, cache_keys[:, column], preferred_element_ty...]
    reduce_sum x3 -> x1, other arithmetic: 4.74 us -> 0.91 us  [local(): slot = target * 2 + jnp.sum(earlier.astype(jnp.int32), axis=1)]
    unnamed x19 -> x12, local copies, waits for them, and re-layouts: 3.38 us -> 6.73 us
    scatter x1 -> x0, local copies, waits for them, and re-layouts: 2.21 us -> none  [local(): jnp.zeros((sections * most, BLOCK_TOK, 2, kv_width), jnp.bfloat16).at[index]]
    convert_element_type x4 -> x1, other arithmetic: 2.5 us -> 0.66 us  [local(): jnp.tile(jnp.repeat(slot, BLOCK_TOK), 2 * KV_WIDTH // ROWS)]
  transfers between devices with their start and end apart: 3 -> 0, of which waited for: 2 -> 0; matrix products, arithmetic and copies ran while one was open for 4% -> 0% of each run, Pallas kernels for 0% -> 0%
where the time goes in v1:
time: 69.6 us; the launch traced here: 68.9 us
  Pallas kernels  58.5 us (84%)
  local copies, waits for them, and re-layouts  6.91 us (10%)
  other arithmetic  2.01 us (3%)
  between operations  1.41 us (2%)
    pallas_call x1, Pallas kernels, local(): pl.pallas_call(kernel, out_shape=(jax.ShapeDtypeStruct((ROW_PART, TENSOR...  58.5 us
    unnamed x12, local copies, waits for them, and re-layouts  6.73 us

profile of v1, /device:TPU:1, one launch (start us, length us, event | category | flops | bytes accessed | tf_op | source)
XLA Modules:
  0.0 68.9 jit_solution(2107436913977955188)
XLA Ops:
  0.6 0.0 copy-start.1
  1.4 0.9 %convert_reduce_fusion = s32[16]{0:T(128)S(1)} fusion(s32[16]{0:T(128)} %bitcast.9), kind=kLoop, calls=%fused_computation.6 | loop fusion | flops 1264 | bytes 128 | tf_op jit(solution)/shard_map/reduce_sum | solution.py:170
  2.3 0.7 add_convert_fusion
  2.9 0.1 broadcast_in_dim.24
  3.0 0.1 convert_element_type.24
  3.2 0.3 fusion
  3.5 0.1 pad_maximum_fusion
  3.6 0.0 copy-done.1
  3.6 0.0 copy-start
  3.6 1.2 %copy-done = bf16[128,4096]{1,0:T(8,128)(2,1)S(1)} copy-done((bf16[128,4096]{1,0:T(8,128)(2,1)S(1)}, bf16[128,4096]{1,0:T(8,128)(2,1)}, u32[]{:S(2)}) %copy-start) | copy-done | bytes 1048600
  4.8 0.0 copy-start.2
  4.8 1.0 %copy-done.2 = bf16[1024,256]{1,0:T(8,128)(2,1)S(1)} copy-done((bf16[1024,256]{1,0:T(8,128)(2,1)S(1)}, bf16[1024,256]{1,0:T(8,128)(2,1)}, u32[]{:S(2)}) %copy-start.2) | copy-done | bytes 524312
  5.9 0.0 copy-start.3
  5.9 0.8 %copy-done.3 = bf16[128,256]{1,0:T(8,128)(2,1)S(1)} copy-done((bf16[128,256]{1,0:T(8,128)(2,1)S(1)}, bf16[128,256]{1,0:T(8,128)(2,1)}, u32[]{:S(2)}) %copy-start.3) | copy-done | bytes 65560
  6.7 0.0 copy-start.4
  6.7 0.8 %copy-done.4 = bf16[128,256]{1,0:T(8,128)(2,1)S(1)} copy-done((bf16[128,256]{1,0:T(8,128)(2,1)S(1)}, bf16[128,256]{1,0:T(8,128)(2,1)}, u32[]{:S(2)}) %copy-start.4) | copy-done | bytes 65560
  7.5 58.5 %spanned.1 = (bf16[32,16384]{1,0:T(8,128)(2,1)S(1)}, bf16[4,16,16,512]{3,2,1,0:T(8,128)(2,1)S(1)}) custom-call(bf16[128,4096]{1,0:T(8,128)(2,1)S(1)} %copy-done, bf16[128,256]{1,0:T(8,128)(2,1)S(1)} %copy-done.3, bf16[128,256]{1,0:T(8,128)(2,1)S(1)} %copy-done.4, bf16[1024,256]{1,0:T(8,128)(2,1)S(1)} %copy-done.1, bf16[1024,256]{1,0:T(8,128)(2,1)S(1)} %copy-done.2, ...), custom_call_target="tpu_custom_call" | custom-call | tf_op jit(solution)/shard_map/spanned/pallas_call | solution.py:175
  66.1 1.8 %copy.11 = bf16[128,8,2,256]{3,2,1,0:T(2,128)(2,1)} copy(bf16[128,8,2,256]{3,1,2,0:T(8,128)(2,1)S(1)} %bitcast.8) | data formatting | bytes 2097152
  67.9 1.0 %copy.14 = bf16[32,16384]{1,0:T(8,128)(2,1)} copy(bf16[32,16384]{1,0:T(8,128)(2,1)S(1)} %get-tuple-element.19) | data formatting | bytes 2097152
  (5 shorter events, 0.0 us)
Async XLA Ops:
  0.6 3.0 %copy-start.1 = (bf16[1024,256]{1,0:T(8,128)(2,1)S(1)}, bf16[1024,256]{1,0:T(8,128)(2,1)}, u32[]{:S(2)}) copy-start(bf16[1024,256]{1,0:T(8,128)(2,1)} %cache_keys.1) | copy-start | bytes 1572868
  3.6 1.2 %copy-start = (bf16[128,4096]{1,0:T(8,128)(2,1)S(1)}, bf16[128,4096]{1,0:T(8,128)(2,1)}, u32[]{:S(2)}) copy-start(bf16[128,4096]{1,0:T(8,128)(2,1)} %queries.1) | copy-start | bytes 3145732
  4.8 1.0 %copy-start.2 = (bf16[1024,256]{1,0:T(8,128)(2,1)S(1)}, bf16[1024,256]{1,0:T(8,128)(2,1)}, u32[]{:S(2)}) copy-start(bf16[1024,256]{1,0:T(8,128)(2,1)} %cache_values.1) | copy-start | bytes 1572868
  5.9 0.8 %copy-start.3 = (bf16[128,256]{1,0:T(8,128)(2,1)S(1)}, bf16[128,256]{1,0:T(8,128)(2,1)}, u32[]{:S(2)}) copy-start(bf16[128,256]{1,0:T(8,128)(2,1)} %new_keys.1) | copy-start | bytes 196612
  6.7 0.8 %copy-start.4 = (bf16[128,256]{1,0:T(8,128)(2,1)S(1)}, bf16[128,256]{1,0:T(8,128)(2,1)}, u32[]{:S(2)}) copy-start(bf16[128,256]{1,0:T(8,128)(2,1)} %new_values.1) | copy-start | bytes 196612

commit v2 on v1

v2 whole, which is shorter than its diff:
```python
import functools

import jax
import jax.numpy as jnp
from jax import lax
from jax.experimental import pallas as pl
from jax.experimental.pallas import tpu as pltpu
from jax.sharding import PartitionSpec as P

MESH = pl.DeviceIdType.MESH
HEAD = 128
ROWS = 128
CACHE = 1024
BLOCK_TOK = 8
BLOCKS = ROWS // BLOCK_TOK
PLANE = 16
DEPTH = 4
TENSOR = 4
HEADS = 32
WIDTH = HEADS * HEAD
STEP_HEADS = 4
STEPS = HEADS // STEP_HEADS
STEP_COLS = STEP_HEADS * HEAD
KV_WIDTH = 2 * HEAD
ROW_PART = ROWS // TENSOR
ARRIVAL = 32
AROUND = 2
AROUND_COLS = AROUND * STEP_COLS
MASKED = -1e30
LAG = 3
PASS_AT = 5
ARRIVALS = (2, 4, 6)


def kernel(
    length, placement, queries_hbm, new_keys_hbm, new_values_hbm, cache_keys_hbm, cache_values_hbm,
    handed, landed,
    queries, new_keys, cache_keys, cache_values, cosine, sine, bias, attended, held, packed, passing,
    load_sem, in_send, in_recv, plane_send, plane_recv, own_sem, out_send, out_recv, pass_recv, pass_send,
):
    section = lax.axis_index("section")
    tensor = lax.axis_index("tensor")
    sections = DEPTH * PLANE
    z, xy = section // PLANE, section % PLANE
    core = tensor % 2
    after = lax.rem(section + 1, sections)
    before = lax.rem(section + sections - 1, sections)
    height = tensor // 2 * DEPTH + z
    turning = xy == PLANE - 1

    def at(plane_index, level, core_index):
        level = lax.rem(level, 2 * DEPTH)
        return (lax.rem(level, DEPTH) * PLANE + plane_index, level // DEPTH * 2 + core_index)

    barrier = pltpu.get_barrier_semaphore()

    def greet(device):
        pl.semaphore_signal(barrier, inc=1, device_id=device, device_id_type=MESH)

    for i in range(1, DEPTH):
        greet((lax.rem(z + i, DEPTH) * PLANE + xy, tensor))
    for i in range(TENSOR):
        greet((before, lax.rem(tensor + i, TENSOR)))

    @pl.loop(1, PLANE)
    def _(i):
        greet((z * PLANE + lax.rem(xy + i, PLANE), tensor))

    @pl.when(turning)
    def _():
        greet(at(xy, height + 6, core))

    @pl.when(xy == 0)
    def _():
        for i in range(2):
            greet(at(PLANE - 1, height + 5, i))

    loads = [
        pltpu.make_async_copy(new_keys_hbm, new_keys, load_sem.at[0]),
        pltpu.make_async_copy(new_values_hbm, held.at[z, pl.ds(ROWS, ROWS)], load_sem.at[1]),
        pltpu.make_async_copy(cache_keys_hbm, cache_keys, load_sem.at[2]),
        pltpu.make_async_copy(queries_hbm, queries, load_sem.at[3]),
        pltpu.make_async_copy(cache_values_hbm, cache_values, load_sem.at[4]),
    ]
    for load in loads:
        load.start()

    row = lax.broadcasted_iota(jnp.int32, (ROWS, ROWS), 0)
    column = lax.broadcasted_iota(jnp.int32, (ROWS, ROWS), 1)
    live = length[0]
    index = (column % (HEAD // 2)).astype(jnp.float32)
    frequency = jnp.exp(index[0:8] * (-2.0 / HEAD) * jnp.log(jnp.float32(500000.0)))[0:1]
    angles = (live.astype(jnp.float32) + row.astype(jnp.float32)) * frequency
    cosine[...] = jnp.cos(angles)
    sine[...] = jnp.where(column < HEAD // 2, -1.0, 1.0) * jnp.sin(angles)
    bias[...] = jnp.where(lax.broadcasted_iota(jnp.int32, (1, CACHE), 1) < live, 0.0, MASKED)

    block = lax.broadcasted_iota(jnp.int32, (16, ROWS), 1) // BLOCK_TOK
    target = jnp.zeros((16, ROWS), jnp.int32)
    for b in range(BLOCKS):
        target = jnp.where(block == b, placement[0, b], target)
    slot = target * 2
    for b in range(BLOCKS):
        slot = slot + jnp.where((target == placement[0, b]) & (block > b), 1, 0)
    slot = slot.astype(jnp.float32).astype(jnp.bfloat16)
    held[z, pl.ds(2 * ROWS, 16), :] = jnp.concatenate([slot, slot], axis=1)

    def rotate(part):
        part = part.astype(jnp.float32)
        turned = pltpu.roll(part, HEAD // 2, 1)
        return (part * cosine[...] + turned * sine[...]).astype(jnp.bfloat16)

    loads[0].wait()
    for g in range(2):
        columns = pl.ds(g * HEAD, HEAD)
        held[z, pl.ds(0, ROWS), columns] = rotate(new_keys[:, columns])
    loads[1].wait()

    pl.semaphore_wait(barrier, DEPTH - 1 + TENSOR + PLANE - 1 + jnp.where(turning, 3, 0))

    inner = z % 3 > 0
    nearest = 1 + z % 2
    farthest = jnp.where(z < 2, DEPTH - 1, 0)
    middle = 6 - z - nearest - farthest
    edge = jnp.where(z < 2, 0, DEPTH - 1)

    def gather(source, level):
        pltpu.make_async_remote_copy(
            src_ref=held.at[source], dst_ref=held.at[source], send_sem=in_send, recv_sem=in_recv.at[source],
            device_id=(level * PLANE + xy, tensor), device_id_type=MESH,
        ).start()

    gather(z, nearest)
    gather(z, middle)

    def spread(source):
        tall = PLANE * ARRIVAL
        row = lax.broadcasted_iota(jnp.int32, (tall, ROWS), 0)
        column = lax.broadcasted_iota(jnp.int32, (tall, ROWS), 1)
        slot = held[source, pl.ds(2 * ROWS, 16), pl.ds(0, ROWS)].astype(jnp.float32)[0:1, :]
        wanted = (row // 16 + z * (PLANE * 2)).astype(jnp.float32)
        here = (slot == wanted) & (row % 16 // 2 == column % BLOCK_TOK)
        picked = jnp.concatenate(
            [jnp.where(here & (row % 2 == k), 1.0, 0.0) for k in range(2)], axis=1
        ).astype(jnp.bfloat16)
        moved = jnp.dot(picked, held[source, pl.ds(0, 2 * ROWS), :], preferred_element_type=jnp.float32)
        packed[source] = moved.astype(jnp.bfloat16).reshape(PLANE, ARRIVAL // 2, 2, KV_WIDTH)

        @pl.loop(1, PLANE)
        def _(i):
            other = lax.rem(xy + i, PLANE)
            pltpu.make_async_remote_copy(
                src_ref=packed.at[source, other], dst_ref=landed.at[source, xy],
                send_sem=plane_send, recv_sem=plane_recv,
                device_id=(z * PLANE + other, tensor), device_id_type=MESH,
            ).start()
        pltpu.make_async_copy(packed.at[source, xy], landed.at[source, xy], own_sem).start()

    spread(z)

    for load in loads[2:]:
        load.wait()
    causal = column <= row
    sharp = HEAD ** (-0.5) * 1.4426950408889634
    far = (height + 5) % (2 * DEPTH) // DEPTH * 2

    def hand(part, start, count):
        start = pl.multiple_of(start, STEP_COLS)
        pltpu.make_async_remote_copy(
            src_ref=attended.at[
                pl.ds(pl.multiple_of(part * ROW_PART, ROW_PART), ROW_PART), pl.ds(start, count)
            ],
            dst_ref=handed.at[:, pl.ds(pl.multiple_of(tensor * WIDTH + start, STEP_COLS), count)],
            send_sem=out_send, recv_sem=out_recv,
            device_id=(after, part), device_id_type=MESH,
        ).start()

    crossing = 2 - tensor // 2 * 2
    split = turning & (z < DEPTH - 1)

    def drain(ref, sem):
        pltpu.make_async_copy(ref, ref, sem).wait()

    @pl.loop(0, STEPS)
    def _(step):
        g = step // (STEPS // 2)
        kv_columns = pl.ds(pl.multiple_of(g * HEAD, HEAD), HEAD)
        base = step * STEP_COLS
        dims = (((1,), (1,)), ((), ()))
        for h in range(STEP_HEADS):
            columns = pl.ds(pl.multiple_of(base + h * HEAD, HEAD), HEAD)
            query = rotate(queries[:, columns])
            old = lax.dot_general(query, cache_keys[:, kv_columns], dims, preferred_element_type=jnp.float32)
            new = lax.dot_general(
                query, held[z, pl.ds(0, ROWS), kv_columns], dims, preferred_element_type=jnp.float32
            )
            old = old + bias[...]
            new = jnp.where(causal, new, MASKED)
            top = jnp.maximum(jnp.max(old, axis=1, keepdims=True), jnp.max(new, axis=1, keepdims=True))
            old = jnp.exp2((old - top) * sharp)
            new = jnp.exp2((new - top) * sharp)
            total = jnp.sum(old, axis=1, keepdims=True) + jnp.sum(new, axis=1, keepdims=True)
            summed = jnp.dot(
                old.astype(jnp.bfloat16), cache_values[:, kv_columns], preferred_element_type=jnp.float32
            ) + jnp.dot(
                new.astype(jnp.bfloat16), held[z, pl.ds(ROWS, ROWS), kv_columns],
                preferred_element_type=jnp.float32,
            )
            attended[:, columns] = (summed / total).astype(jnp.bfloat16)

        around = turning & (step < AROUND)

        @pl.when(around)
        def _():
            for i in range(2):
                part = far + i
                pltpu.make_async_remote_copy(
                    src_ref=attended.at[
                        pl.ds(pl.multiple_of(part * ROW_PART, ROW_PART), ROW_PART),
                        pl.ds(pl.multiple_of(base, STEP_COLS), STEP_COLS),
                    ],
                    dst_ref=passing.at[i, :, pl.ds(pl.multiple_of(base, STEP_COLS), STEP_COLS)],
                    send_sem=out_send, recv_sem=pass_recv,
                    device_id=at(xy, height + 2, core), device_id_type=MESH,
                ).start()

        @pl.when(jnp.logical_not(around & (z == DEPTH - 1)))
        def _():
            for i in range(2):
                hand(tensor // 2 * 2 + i, base, STEP_COLS)

        @pl.when((step == LAG) & split)
        def _():
            for i in range(2):
                hand(crossing + i, AROUND_COLS, LAG * STEP_COLS - AROUND_COLS)

        @pl.when((step == LAG) & jnp.logical_not(split))
        def _():
            for i in range(2):
                hand(crossing + i, 0, LAG * STEP_COLS)

        @pl.when(step >= LAG)
        def _():
            for i in range(2):
                hand(crossing + i, base, STEP_COLS)

        @pl.when(turning & (step == PASS_AT))
        def _():
            drain(passing, pass_recv)
            first = lax.rem(height + 6, 2 * DEPTH)
            owner = first // DEPTH * 2 + core
            goal = lax.rem(lax.rem(first, DEPTH) * PLANE + PLANE, sections)
            for i in range(2):
                part = lax.rem(first + 5, 2 * DEPTH) // DEPTH * 2 + i
                pltpu.make_async_remote_copy(
                    src_ref=passing.at[i],
                    dst_ref=handed.at[:, pl.ds(pl.multiple_of(owner * WIDTH, WIDTH), AROUND_COLS)],
                    send_sem=pass_send, recv_sem=out_recv,
                    device_id=(goal, part), device_id_type=MESH,
                ).start()

        sources = (nearest, jnp.where(inner, farthest, middle), jnp.where(inner, middle, farthest))
        for n, when in enumerate(ARRIVALS):
            @pl.when(step == when)
            def _(n=n):
                source = sources[n]
                pltpu.make_async_copy(held.at[source], held.at[source], in_recv.at[source]).wait()
                if n < 2:
                    @pl.when(inner)
                    def _():
                        gather(source, edge)
                spread(source)

    drain(held.at[pl.ds(0, 2)], in_send)

    @pl.when(inner)
    def _():
        drain(held.at[pl.ds(0, 2)], in_send)

    drain(packed.at[:, 0], own_sem)
    drain(packed.at[:, pl.ds(0, PLANE - 1)], plane_send)
    drain(landed.at[:, pl.ds(0, PLANE - 1)], plane_recv)
    drain(attended, out_send)

    @pl.when(turning)
    def _():
        drain(passing, pass_send)

    drain(handed, out_recv)


def local(queries, new_keys, new_values, cache_keys, cache_values, prior_length, placement):
    vmem = pl.BlockSpec(memory_space=pltpu.VMEM)
    smem = pl.BlockSpec(memory_space=pltpu.SMEM)
    hbm = pl.BlockSpec(memory_space=pltpu.HBM)
    half = jnp.bfloat16
    handed, landed = pl.pallas_call(
        kernel,
        out_shape=(
            pltpu.VMEM((ROW_PART, TENSOR * WIDTH), half),
            pltpu.VMEM((DEPTH, PLANE, ARRIVAL // 2, 2, KV_WIDTH), half),
        ),
        in_specs=[smem] * 2 + [hbm] * 5,
        out_specs=(vmem, vmem),
        scratch_shapes=[
            pltpu.VMEM((ROWS, WIDTH), half),
            pltpu.VMEM((ROWS, KV_WIDTH), half),
            pltpu.VMEM((CACHE, KV_WIDTH), half),
            pltpu.VMEM((CACHE, KV_WIDTH), half),
            pltpu.VMEM((ROWS, HEAD), jnp.float32),
            pltpu.VMEM((ROWS, HEAD), jnp.float32),
            pltpu.VMEM((1, CACHE), jnp.float32),
            pltpu.VMEM((ROWS, WIDTH), half),
            pltpu.VMEM((DEPTH, 2 * ROWS + 16, KV_WIDTH), half),
            pltpu.VMEM((DEPTH, PLANE, ARRIVAL // 2, 2, KV_WIDTH), half),
            pltpu.VMEM((2, ROW_PART, AROUND_COLS), half),
            pltpu.SemaphoreType.DMA((5,)),
            pltpu.SemaphoreType.DMA,
            pltpu.SemaphoreType.DMA((DEPTH,)),
        ]
        + [pltpu.SemaphoreType.DMA] * 7,
        compiler_params=pltpu.CompilerParams(
            collective_id=0, has_side_effects=True, vmem_limit_bytes=60 << 20
        ),
        name="spanned",
    )(prior_length, placement.reshape(1, BLOCKS), queries, new_keys, new_values, cache_keys, cache_values)
    return handed, landed.reshape(DEPTH * PLANE * 2, BLOCK_TOK, 2, KV_WIDTH)


def solution(mesh):
    placed = (
        P("section", "tensor"),
        P("section", "tensor"),
        P("section", "tensor"),
        P("section", "tensor"),
        P("section", "tensor"),
        P("section"),
        P("section", None),
    )
    return jax.shard_map(
        local,
        mesh=mesh,
        in_specs=placed,
        out_specs=(P(("section", "tensor"), None), P("section", None, None, "tensor")),
        check_vma=False,
    )
```

time: 69.6 us -> 57.6 us (0.83)
  the two profiles are of different devices: /device:TPU:1 before, /device:TPU:33 now
where the time goes in v2:
time: 57.6 us; the launch traced here: 57.5 us
  Pallas kernels  54.3 us (94%)
  local copies, waits for them, and re-layouts  1.94 us (3%)
  between operations  1.29 us (2%)
    pallas_call x1, Pallas kernels, local(): pl.pallas_call(kernel, out_shape=(pltpu.VMEM((ROW_PART, TENSOR * WIDTH),...  54.3 us
    unnamed x2, local copies, waits for them, and re-layouts  1.94 us

profile of v2, /device:TPU:33, one launch (start us, length us, event | category | flops | bytes accessed | tf_op | source)
XLA Modules:
  0.0 57.5 jit_solution(11839901662879447406)
XLA Ops:
  1.3 54.3 %spanned.1 = (bf16[32,16384]{1,0:T(8,128)(2,1)S(1)}, bf16[4,16,16,2,256]{4,3,2,1,0:T(2,128)(2,1)S(1)}) custom-call(s32[1]{0:T(128)S(6)} %copy.13.length, s32[1,16]{1,0:T(1,128)} %bitcast.3, bf16[128,4096]{1,0:T(8,128)(2,1)} %queries_hbm.1, bf16[128,256]{1,0:T(8,128)(2,1)} %new_keys_hbm.1, bf16[128,256]{1,0:T(8,128)(2,1)} %new_values_hbm.1, ...), custom_call_target="tpu_custom_call" | custom-call | tf_op jit(solution)/shard_map/spanned/pallas_call | solution.py:297
  55.6 1.0 %copy.11 = bf16[32,16384]{1,0:T(8,128)(2,1)} copy(bf16[32,16384]{1,0:T(8,128)(2,1)S(1)} %get-tuple-element.6) | data formatting | bytes 2097152
  56.6 1.0 %copy.12 = bf16[128,8,2,256]{3,2,1,0:T(2,128)(2,1)} copy(bf16[128,8,2,256]{3,2,1,0:T(2,128)(2,1)S(1)} %bitcast.2) | data formatting | bytes 2097152

commit v3 on v2

--- a/solution.py
+++ b/solution.py
@@ -24,12 +24,10 @@
 KV_WIDTH = 2 * HEAD
 ROW_PART = ROWS // TENSOR
 ARRIVAL = 32
-AROUND = 2
-AROUND_COLS = AROUND * STEP_COLS
+AROUND = 3
 MASKED = -1e30
 LAG = 3
-PASS_AT = 5
-ARRIVALS = (2, 4, 6)
+ARRIVALS = (1, 2, 4)
 
 
 def kernel(
@@ -47,6 +45,7 @@
     before = lax.rem(section + sections - 1, sections)
     height = tensor // 2 * DEPTH + z
     turning = xy == PLANE - 1
+    relaying = (xy > 0) & (xy <= 2 * AROUND)
 
     def at(plane_index, level, core_index):
         level = lax.rem(level, 2 * DEPTH)
@@ -66,14 +65,15 @@
     def _(i):
         greet((z * PLANE + lax.rem(xy + i, PLANE), tensor))
 
-    @pl.when(turning)
-    def _():
-        greet(at(xy, height + 6, core))
+    @pl.when(relaying)
+    def _():
+        greet(at(PLANE - 1, height, core))
 
     @pl.when(xy == 0)
     def _():
-        for i in range(2):
-            greet(at(PLANE - 1, height + 5, i))
+        for i in range(AROUND):
+            for k in range(2):
+                greet(at(2 * i + core + 1, height + 3, k))
 
     loads = [
         pltpu.make_async_copy(new_keys_hbm, new_keys, load_sem.at[0]),
@@ -116,7 +116,8 @@
         held[z, pl.ds(0, ROWS), columns] = rotate(new_keys[:, columns])
     loads[1].wait()
 
-    pl.semaphore_wait(barrier, DEPTH - 1 + TENSOR + PLANE - 1 + jnp.where(turning, 3, 0))
+    extra = jnp.where(turning, 2 * AROUND, 0) + jnp.where(relaying, 1, 0)
+    pl.semaphore_wait(barrier, DEPTH - 1 + TENSOR + PLANE - 1 + extra)
 
     inner = z % 3 > 0
     nearest = 1 + z % 2
@@ -219,9 +220,9 @@
                         pl.ds(pl.multiple_of(part * ROW_PART, ROW_PART), ROW_PART),
                         pl.ds(pl.multiple_of(base, STEP_COLS), STEP_COLS),
                     ],
-                    dst_ref=passing.at[i, :, pl.ds(pl.multiple_of(base, STEP_COLS), STEP_COLS)],
+                    dst_ref=passing,
                     send_sem=out_send, recv_sem=pass_recv,
-                    device_id=at(xy, height + 2, core), device_id_type=MESH,
+                    device_id=at(2 * step + i + 1, height, core), device_id_type=MESH,
                 ).start()
 
         @pl.when(jnp.logical_not(around & (z == DEPTH - 1)))
@@ -229,35 +230,15 @@
             for i in range(2):
                 hand(tensor // 2 * 2 + i, base, STEP_COLS)
 
-        @pl.when((step == LAG) & split)
-        def _():
-            for i in range(2):
-                hand(crossing + i, AROUND_COLS, LAG * STEP_COLS - AROUND_COLS)
-
         @pl.when((step == LAG) & jnp.logical_not(split))
         def _():
             for i in range(2):
                 hand(crossing + i, 0, LAG * STEP_COLS)
 
-        @pl.when(step >= LAG)
+        @pl.when(step >= jnp.where(split, AROUND, LAG))
         def _():
             for i in range(2):
                 hand(crossing + i, base, STEP_COLS)
-
-        @pl.when(turning & (step == PASS_AT))
-        def _():
-            drain(passing, pass_recv)
-            first = lax.rem(height + 6, 2 * DEPTH)
-            owner = first // DEPTH * 2 + core
-            goal = lax.rem(lax.rem(first, DEPTH) * PLANE + PLANE, sections)
-            for i in range(2):
-                part = lax.rem(first + 5, 2 * DEPTH) // DEPTH * 2 + i
-                pltpu.make_async_remote_copy(
-                    src_ref=passing.at[i],
-                    dst_ref=handed.at[:, pl.ds(pl.multiple_of(owner * WIDTH, WIDTH), AROUND_COLS)],
-                    send_sem=pass_send, recv_sem=out_recv,
-                    device_id=(goal, part), device_id_type=MESH,
-                ).start()
 
         sources = (nearest, jnp.where(inner, farthest, middle), jnp.where(inner, middle, farthest))
         for n, when in enumerate(ARRIVALS):
@@ -271,6 +252,17 @@
                         gather(source, edge)
                 spread(source)
 
+    @pl.when(relaying)
+    def _():
+        drain(passing, pass_recv)
+        start = tensor * WIDTH + (xy - 1) // 2 * STEP_COLS
+        pltpu.make_async_remote_copy(
+            src_ref=passing,
+            dst_ref=handed.at[:, pl.ds(pl.multiple_of(start, STEP_COLS), STEP_COLS)],
+            send_sem=pass_send, recv_sem=out_recv,
+            device_id=at(0, height + 5, lax.rem(xy + 1, 2)), device_id_type=MESH,
+        ).start()
+
     drain(held.at[pl.ds(0, 2)], in_send)
 
     @pl.when(inner)
@@ -282,11 +274,22 @@
     drain(landed.at[:, pl.ds(0, PLANE - 1)], plane_recv)
     drain(attended, out_send)
 
-    @pl.when(turning)
+    @pl.when(relaying)
     def _():
         drain(passing, pass_send)
 
     drain(handed, out_recv)
+
+
+def settle(handed, landed, handed_out, landed_out, sem):
+    copies = [
+        pltpu.make_async_copy(landed, landed_out, sem.at[0]),
+        pltpu.make_async_copy(handed, handed_out, sem.at[1]),
+    ]
+    for copy in copies:
+        copy.start()
+    for copy in copies:
+        copy.wait()
 
 
 def local(queries, new_keys, new_values, cache_keys, cache_values, prior_length, placement):
@@ -313,7 +316,7 @@
             pltpu.VMEM((ROWS, WIDTH), half),
             pltpu.VMEM((DEPTH, 2 * ROWS + 16, KV_WIDTH), half),
             pltpu.VMEM((DEPTH, PLANE, ARRIVAL // 2, 2, KV_WIDTH), half),
-            pltpu.VMEM((2, ROW_PART, AROUND_COLS), half),
+            pltpu.VMEM((ROW_PART, STEP_COLS), half),
             pltpu.SemaphoreType.DMA((5,)),
             pltpu.SemaphoreType.DMA,
             pltpu.SemaphoreType.DMA((DEPTH,)),
@@ -324,7 +327,19 @@
         ),
         name="spanned",
     )(prior_length, placement.reshape(1, BLOCKS), queries, new_keys, new_values, cache_keys, cache_values)
-    return handed, landed.reshape(DEPTH * PLANE * 2, BLOCK_TOK, 2, KV_WIDTH)
+    landed = landed.reshape(DEPTH * PLANE * 2, BLOCK_TOK, 2, KV_WIDTH)
+    return pl.pallas_call(
+        settle,
+        out_shape=(
+            jax.ShapeDtypeStruct(handed.shape, half),
+            jax.ShapeDtypeStruct(landed.shape, half),
+        ),
+        in_specs=[vmem] * 2,
+        out_specs=(hbm, hbm),
+        scratch_shapes=[pltpu.SemaphoreType.DMA((2,))],
+        compiler_params=pltpu.CompilerParams(vmem_limit_bytes=8 << 20),
+        name="settle",
+    )(handed, landed)
 
 
 def solution(mesh):

time: 57.6 us -> 51.9 us (0.901)
  the two profiles are of different devices: /device:TPU:33 before, /device:TPU:1 now
where the time goes in v3:
time: 51.9 us; the launch traced here: 51.8 us
  Pallas kernels  50.5 us (97%)
  between operations  1.29 us (2%)
    pallas_call x1, Pallas kernels, local(): pl.pallas_call(kernel, out_shape=(pltpu.VMEM((ROW_PART, TENSOR * WIDTH),...  49.2 us
    pallas_call x1, Pallas kernels, local(): pl.pallas_call(settle, out_shape=(jax.ShapeDtypeStruct(handed.shape, half...  1.33 us

profile of v3, /device:TPU:1, one launch (start us, length us, event | category | flops | bytes accessed | tf_op | source)
XLA Modules:
  0.0 51.8 jit_solution(5578973103611641958)
XLA Ops:
  1.3 49.2 %spanned.1 = (bf16[32,16384]{1,0:T(8,128)(2,1)S(1)}, bf16[4,16,16,2,256]{4,3,2,1,0:T(2,128)(2,1)S(1)}) custom-call(s32[1]{0:T(128)S(6)} %copy.9.length, s32[1,16]{1,0:T(1,128)} %bitcast.3, bf16[128,4096]{1,0:T(8,128)(2,1)} %queries_hbm.1, bf16[128,256]{1,0:T(8,128)(2,1)} %new_keys_hbm.1, bf16[128,256]{1,0:T(8,128)(2,1)} %new_values_hbm.1, ...), custom_call_target="tpu_custom_call" | custom-call | tf_op jit(solution)/shard_map/spanned/pallas_call | solution.py:300
  50.5 1.3 %settle.1 = (bf16[32,16384]{1,0:T(8,128)(2,1)}, bf16[128,8,2,256]{3,2,1,0:T(2,128)(2,1)}) custom-call(bf16[32,16384]{1,0:T(8,128)(2,1)S(1)} %get-tuple-element.4.handed, bf16[128,8,2,256]{3,2,1,0:T(2,128)(2,1)S(1)} %bitcast.2), custom_call_target="tpu_custom_call" | custom-call | tf_op jit(solution)/shard_map/settle/pallas_call | solution.py:331

commit v4 on v3

--- a/solution.py
+++ b/solution.py
@@ -1,5 +1,3 @@
-import functools
-
 import jax
 import jax.numpy as jnp
 from jax import lax
@@ -26,14 +24,14 @@
 ARRIVAL = 32
 AROUND = 3
 MASKED = -1e30
-LAG = 3
-ARRIVALS = (1, 2, 4)
+LAG = 5
+ARRIVALS = (1, 3, 5)
 
 
 def kernel(
-    length, placement, queries_hbm, new_keys_hbm, new_values_hbm, cache_keys_hbm, cache_values_hbm,
+    length, placement_hbm, queries_hbm, new_keys_hbm, new_values_hbm, cache_keys_hbm, cache_values_hbm,
     handed, landed,
-    queries, new_keys, cache_keys, cache_values, cosine, sine, bias, attended, held, packed, passing,
+    placement, queries, new_keys, cache_keys, cache_values, cosine, sine, bias, attended, held, packed, passing,
     load_sem, in_send, in_recv, plane_send, plane_recv, own_sem, out_send, out_recv, pass_recv, pass_send,
 ):
     section = lax.axis_index("section")
@@ -81,9 +79,12 @@
         pltpu.make_async_copy(cache_keys_hbm, cache_keys, load_sem.at[2]),
         pltpu.make_async_copy(queries_hbm, queries, load_sem.at[3]),
         pltpu.make_async_copy(cache_values_hbm, cache_values, load_sem.at[4]),
+        pltpu.make_async_copy(placement_hbm, placement, load_sem.at[5]),
     ]
-    for load in loads:
+    for load in loads[5:] + loads[:5]:
         load.start()
+    for load in loads[5:]:
+        load.wait()
 
     row = lax.broadcasted_iota(jnp.int32, (ROWS, ROWS), 0)
     column = lax.broadcasted_iota(jnp.int32, (ROWS, ROWS), 1)
@@ -159,7 +160,7 @@
 
     spread(z)
 
-    for load in loads[2:]:
+    for load in loads[2:5]:
         load.wait()
     causal = column <= row
     sharp = HEAD ** (-0.5) * 1.4426950408889634
@@ -188,6 +189,7 @@
         kv_columns = pl.ds(pl.multiple_of(g * HEAD, HEAD), HEAD)
         base = step * STEP_COLS
         dims = (((1,), (1,)), ((), ()))
+        rows_of = []
         for h in range(STEP_HEADS):
             columns = pl.ds(pl.multiple_of(base + h * HEAD, HEAD), HEAD)
             query = rotate(queries[:, columns])
@@ -195,8 +197,8 @@
             new = lax.dot_general(
                 query, held[z, pl.ds(0, ROWS), kv_columns], dims, preferred_element_type=jnp.float32
             )
-            old = old + bias[...]
-            new = jnp.where(causal, new, MASKED)
+            rows_of.append((columns, old + bias[...], jnp.where(causal, new, MASKED)))
+        for columns, old, new in rows_of:
             top = jnp.maximum(jnp.max(old, axis=1, keepdims=True), jnp.max(new, axis=1, keepdims=True))
             old = jnp.exp2((old - top) * sharp)
             new = jnp.exp2((new - top) * sharp)
@@ -303,9 +305,10 @@
             pltpu.VMEM((ROW_PART, TENSOR * WIDTH), half),
             pltpu.VMEM((DEPTH, PLANE, ARRIVAL // 2, 2, KV_WIDTH), half),
         ),
-        in_specs=[smem] * 2 + [hbm] * 5,
+        in_specs=[smem] + [hbm] * 6,
         out_specs=(vmem, vmem),
         scratch_shapes=[
+            pltpu.SMEM((1, BLOCKS), jnp.int32),
             pltpu.VMEM((ROWS, WIDTH), half),
             pltpu.VMEM((ROWS, KV_WIDTH), half),
             pltpu.VMEM((CACHE, KV_WIDTH), half),
@@ -317,7 +320,7 @@
             pltpu.VMEM((DEPTH, 2 * ROWS + 16, KV_WIDTH), half),
             pltpu.VMEM((DEPTH, PLANE, ARRIVAL // 2, 2, KV_WIDTH), half),
             pltpu.VMEM((ROW_PART, STEP_COLS), half),
-            pltpu.SemaphoreType.DMA((5,)),
+            pltpu.SemaphoreType.DMA((6,)),
             pltpu.SemaphoreType.DMA,
             pltpu.SemaphoreType.DMA((DEPTH,)),
         ]

time: 51.9 us -> 51.4 us (level); the launches traced: 51.8 us -> 50.4 us
  Pallas kernels: 50.5 us -> 49.2 us
    pallas_call x1, Pallas kernels: 49.2 us -> 47.8 us  [local(): pl.pallas_call(kernel, out_shape=(pltpu.VMEM((ROW_PART, TENSOR * WIDTH),...]
where the time goes in v4:
time: 51.4 us; the launch traced here: 50.4 us
  Pallas kernels  49.2 us (96%)
  between operations  1.29 us (3%)
    pallas_call x1, Pallas kernels, local(): pl.pallas_call(kernel, out_shape=(pltpu.VMEM((ROW_PART, TENSOR * WIDTH),...  47.8 us
    pallas_call x1, Pallas kernels, local(): pl.pallas_call(settle, out_shape=(jax.ShapeDtypeStruct(handed.shape, half...  1.33 us

profile of v4, /device:TPU:1, one launch (start us, length us, event | category | flops | bytes accessed | tf_op | source)
XLA Modules:
  0.0 50.4 jit_solution(3121066291513850481)
XLA Ops:
  1.3 47.8 %spanned.1 = (bf16[32,16384]{1,0:T(8,128)(2,1)S(1)}, bf16[4,16,16,2,256]{4,3,2,1,0:T(2,128)(2,1)S(1)}) custom-call(s32[1]{0:T(128)S(6)} %copy.9.length, s32[1,16]{1,0:T(1,128)} %bitcast.3, bf16[128,4096]{1,0:T(8,128)(2,1)} %queries_hbm.1, bf16[128,256]{1,0:T(8,128)(2,1)} %new_keys_hbm.1, bf16[128,256]{1,0:T(8,128)(2,1)} %new_values_hbm.1, ...), custom_call_target="tpu_custom_call" | custom-call | tf_op jit(solution)/shard_map/spanned/pallas_call | solution.py:302
  49.1 1.3 %settle.1 = (bf16[32,16384]{1,0:T(8,128)(2,1)}, bf16[128,8,2,256]{3,2,1,0:T(2,128)(2,1)}) custom-call(bf16[32,16384]{1,0:T(8,128)(2,1)S(1)} %get-tuple-element.4.handed, bf16[128,8,2,256]{3,2,1,0:T(2,128)(2,1)S(1)} %bitcast.2), custom_call_target="tpu_custom_call" | custom-call | tf_op jit(solution)/shard_map/settle/pallas_call | solution.py:334
